TPU v7x, 32 devices: a whole 2x2x4 slice. The times are simulated.
32 devices in a mesh: rep: 8 (over z, y), tp: 4 (over x, core).
Axes of the slice: x: 2, y: 2, z: 4, core: 2. Of those that a mesh axis runs over, the one named last changes fastest.
Arguments:
- hidden: bfloat16 [8192, 2560], P(('rep', 'tp')), may hold values from -6 to 6
- cotangent: bfloat16 [8192, 512], P('rep', 'tp'), may hold values from -6 to 6
- numerator: float32 [8, 2560, 512], P('rep', None, 'tp'), may hold values from -0.125 to 0.125
- push_weight: float32 [8], P('rep'), as said below
- moment_one: float32 [8, 2560, 512], P('rep', None, 'tp'), may hold values from -180 to 180
- moment_two: float32 [8, 2560, 512], P('rep', None, 'tp'), may hold values from 100 to 10000
- gossip_round: int32 [3], replicated, may hold values from 0 to 2, as said below
Outputs:
- numerator_out: float32 [8, 2560, 512], P('rep', None, 'tp')
- weight_out: float32 [8], P('rep')
- moment_one_out: float32 [8, 2560, 512], P('rep', None, 'tp')
- moment_two_out: float32 [8, 2560, 512], P('rep', None, 'tp')
- values: bfloat16 [8192, 512], P('rep', 'tp')
- grad_hidden: bfloat16 [8192, 2560], P(('rep', 'tp'))
Inputs may be any that keep to these rules, and one draw needn't show every extreme that they name: `gossip_round`: each of the rounds 0, 1, 2 once. `push_weight`: positive.
All inputs are finite; a program needn't handle non-finite values.
Results may differ from a plain program's by a relative error of at most 0.015.
Values may be sent and summed in bfloat16 or wider, within the bound.
A program may use at most 64 MiB of HBM per device.

v0:
```python
import functools

import jax
import jax.numpy as jnp
from jax import lax
from jax.experimental import pallas as pl
from jax.experimental.pallas import tpu as pltpu
from jax.sharding import PartitionSpec as P

MESH = pl.DeviceIdType.MESH
F32 = jnp.float32
BF16 = jnp.bfloat16
ROUNDS = 3
CHUNKS = 5
EARLY = 1


def kernel(
    dist, chunks,
    w_ref, hid_hbm, cot_hbm, num_hbm, m1_hbm, m2_hbm,
    numo_hbm, wo_ref, m1o_hbm, m2o_hbm, val_hbm, gh_hbm,
    hid, num, m1, m2, cot_own, cot_far, nrm, scale,
    deb_own, deb_far, g_own, g_send, g_far, half, half_send, half_far,
    gn, gn_send, gn_near, gh, val_acc, val_own, val_send, w_send, w_far,
    load_sem, write_sem,
    cot_s, cot_r, nrm_s, nrm_r, deb_s, deb_r, g_s, g_r, half_s, half_r, gn_s, gn_r, val_s, val_r, w_s, w_r,
):
    rows, width = hid.shape
    fc = width // chunks
    rep, tp = lax.axis_index("rep"), lax.axis_index("tp")
    n_rep = lax.axis_size("rep")
    near = tp + 1 - 2 * lax.rem(tp, 2)
    far = lax.rem(tp + 2, 4)
    far_near = lax.rem(near + 2, 4)
    to_rep = lax.rem(rep + dist, n_rep)
    from_rep = lax.rem(rep + n_rep - dist, n_rep)
    near_dev, far_dev, to_dev, from_dev = (rep, near), (rep, far), (to_rep, tp), (from_rep, tp)

    def row_block(index):
        return pl.ds(pl.multiple_of(index * rows, rows), rows)

    loads = [
        pltpu.make_async_copy(hid_hbm, hid, load_sem.at[0]),
        pltpu.make_async_copy(num_hbm.at[0], num, load_sem.at[1]),
        pltpu.make_async_copy(cot_hbm.at[row_block(tp)], cot_own.at[pl.ds(0, rows)], load_sem.at[2]),
        pltpu.make_async_copy(cot_hbm.at[row_block(near)], cot_own.at[pl.ds(rows, rows)], load_sem.at[3]),
        pltpu.make_async_copy(m1_hbm.at[0], m1, load_sem.at[4]),
        pltpu.make_async_copy(m2_hbm.at[0], m2, load_sem.at[5]),
    ]
    for load in loads:
        load.start()

    barrier = pltpu.get_barrier_semaphore()
    for device in (near_dev, far_dev, to_dev, from_dev):
        pl.semaphore_signal(barrier, inc=1, device_id=device, device_id_type=MESH)
    pl.semaphore_wait(barrier, 4)

    def remote(src, dst, send, recv, device):
        return pltpu.make_async_remote_copy(
            src_ref=src, dst_ref=dst, send_sem=send, recv_sem=recv, device_id=device, device_id_type=MESH
        )

    cot_copies = [
        remote(cot_hbm.at[row_block(far)], cot_far.at[pl.ds(0, rows)], cot_s.at[0], cot_r.at[0], far_dev),
        remote(cot_hbm.at[row_block(far_near)], cot_far.at[pl.ds(rows, rows)], cot_s.at[1], cot_r.at[1], far_dev),
    ]
    for copy in cot_copies:
        copy.start()
    part = [pl.ds(c * fc, fc) for c in range(chunks)]
    nrm_copies = [
        remote(nrm.at[c, pl.ds(0, rows)], nrm.at[c, pl.ds(rows, rows)], nrm_s.at[c], nrm_r.at[c], near_dev)
        for c in range(chunks)
    ]
    deb_copies = [
        remote(deb_own.at[part[c]], deb_far.at[part[c]], deb_s.at[c], deb_r.at[c], far_dev) for c in range(chunks)
    ]
    g_copies = [
        remote(g_send.at[part[c]], g_far.at[part[c]], g_s.at[c], g_r.at[c], far_dev) for c in range(chunks)
    ]
    half_copies = [
        remote(half_send.at[part[c]], half_far.at[part[c]], half_s.at[c], half_r.at[c], to_dev)
        for c in range(chunks)
    ]
    gn_copies = [
        remote(gn_send.at[c], gn_near.at[c], gn_s.at[c], gn_r.at[c], near_dev) for c in range(chunks)
    ]
    val_copies = [
        remote(val_send.at[pl.ds(0, rows)], val_hbm.at[row_block(tp)], val_s.at[0], val_r.at[0], far_dev),
        remote(val_send.at[pl.ds(rows, rows)], val_hbm.at[row_block(near)], val_s.at[1], val_r.at[1], far_dev),
    ]
    weight = w_ref[0]
    w_send[...] = jnp.full(w_send.shape, weight, F32)
    w_copy = remote(w_send, w_far, w_s.at[0], w_r.at[0], to_dev)
    w_copy.start()

    loads[0].wait()
    step = 32

    @pl.loop(0, rows // step)
    def _(block):
        here = pl.ds(pl.multiple_of(block * step, step), step)
        x = hid[here, :].astype(F32)
        s = lax.rsqrt(jnp.mean(x * x, axis=1, keepdims=True) + 1e-06)
        scale[here, :] = s
        y = (x * s).astype(BF16)
        for c in range(chunks):
            nrm[c, here, :] = y[:, c * fc:(c + 1) * fc]

    for copy in nrm_copies:
        copy.start()

    loads[1].wait()

    def send_deb(c):
        deb_own[part[c], :] = (num[part[c], :] / jnp.full((1, 1), weight, F32)).astype(BF16)
        deb_copies[c].start()

    for c in range(EARLY):
        send_deb(c)

    loads[2].wait()
    loads[3].wait()
    for copy in cot_copies:
        copy.wait_recv()
    cot2 = jnp.concatenate([cot_own[...], cot_far[...]], axis=1)
    k = cot_own.shape[1]
    for c in range(chunks):
        nrm_copies[c].wait_recv()
        p = lax.dot_general(nrm[c], cot2, (((0,), (0,)), ((), ())), preferred_element_type=F32)
        g_send[part[c], :] = p[:, k:].astype(BF16)
        g_copies[c].start()
        g_own[part[c], :] = p[:, :k]
    for c in range(EARLY, chunks):
        send_deb(c)

    loads[4].wait()
    loads[5].wait()
    writes = []

    def write(src, dst):
        copy = pltpu.make_async_copy(src, dst, write_sem.at[len(writes)])
        copy.start()
        writes.append(copy)

    def moments(c):
        g_copies[c].wait_recv()
        here = part[c]
        grad = g_own[here, :] + g_far[here, :].astype(F32)
        first = 0.9 * m1[here, :] + 0.1 * grad
        second = 0.95 * m2[here, :] + 0.05 * grad * grad
        value = num[here, :]
        plain = value / jnp.full((1, 1), weight, F32)
        mine = value - 0.001 * (first / (jnp.sqrt(second) + 1e-08) + 0.1 * plain)
        half_send[here, :] = mine.astype(BF16)
        half_copies[c].start()
        half[here, :] = mine
        m1[here, :] = first
        m2[here, :] = second
        write(m1.at[here], m1o_hbm.at[0, here])
        write(m2.at[here], m2o_hbm.at[0, here])

    def forward(c):
        deb_copies[c].wait_recv()
        here = part[c]
        deb2 = jnp.concatenate([deb_own[here, :], deb_far[here, :]], axis=1)
        dims = (((1,), (1,)), ((), ()))
        both = jnp.concatenate([cot_own[pl.ds(rows, rows), :], cot_far[pl.ds(rows, rows), :]], axis=1)
        gn_send[c] = lax.dot_general(both, deb2, dims, preferred_element_type=F32).astype(BF16)
        gn_copies[c].start()
        product = jnp.dot(nrm[c], deb2, preferred_element_type=F32)
        if c:
            product = val_acc[...] + product
        if c < chunks - 1:
            val_acc[...] = product
        else:
            val_send[...] = product[:, k:].astype(BF16)
            for copy in val_copies:
                copy.start()
            val_own[...] = product[:, :k].astype(BF16)
            write(val_own.at[pl.ds(0, rows)], val_hbm.at[row_block(tp)])
            write(val_own.at[pl.ds(rows, rows)], val_hbm.at[row_block(near)])
        both = jnp.concatenate([cot_own[pl.ds(0, rows), :], cot_far[pl.ds(0, rows), :]], axis=1)
        gn[c] = lax.dot_general(both, deb2, dims, preferred_element_type=F32)

    for c in range(chunks):
        moments(c)
    for c in range(chunks):
        forward(c)

    inner = jnp.zeros((rows, 1), F32)
    for c in range(chunks):
        gn_copies[c].wait_recv()
        total = gn[c] + gn_near[c].astype(F32)
        gn[c] = total
        normal = hid[:, c * fc:(c + 1) * fc].astype(F32) * scale[...]
        inner = inner + jnp.sum(total * normal, axis=1, keepdims=True)
    inner = inner / width
    for c in range(chunks):
        s = scale[...]
        normal = hid[:, c * fc:(c + 1) * fc].astype(F32) * s
        gh[:, c * fc:(c + 1) * fc] = (s * (gn[c] - normal * inner)).astype(BF16)
    write(gh, gh_hbm)

    for c in range(chunks):
        half_copies[c].wait_recv()
        here = part[c]
        num[here, :] = 0.5 * (half[here, :] + half_far[here, :].astype(F32))
        write(num.at[here], numo_hbm.at[0, here])
    w_copy.wait_recv()
    wo_ref[0] = 0.5 * (weight + jnp.max(w_far[...]))

    for copy in val_copies:
        copy.wait_recv()
    for group in (cot_copies, nrm_copies, deb_copies, g_copies, half_copies, gn_copies, val_copies, [w_copy]):
        for copy in group:
            copy.wait_send()
    for copy in writes:
        copy.wait()


def step_of(dist, level, chunks, operands):
    _, hidden, cotangent, numerator, moment_one, moment_two = operands
    rows, width = hidden.shape
    tokens, k = cotangent.shape
    fc = width // chunks
    any_space = pl.BlockSpec(memory_space=pl.ANY)
    smem = pl.BlockSpec(memory_space=pltpu.SMEM)
    dma = pltpu.SemaphoreType.DMA
    full32, full16 = pltpu.VMEM((width, k), F32), pltpu.VMEM((width, k), BF16)
    tok16 = pltpu.VMEM((2 * rows, k), BF16)
    small = pltpu.VMEM((8, 128), F32)
    shapes = [
        jax.ShapeDtypeStruct(numerator.shape, F32),
        jax.ShapeDtypeStruct((1,), F32),
        jax.ShapeDtypeStruct(moment_one.shape, F32),
        jax.ShapeDtypeStruct(moment_two.shape, F32),
        jax.ShapeDtypeStruct((tokens, k), BF16),
        jax.ShapeDtypeStruct((rows, width), BF16),
    ]
    scratch = [
        pltpu.VMEM((rows, width), BF16), full32, full32, full32, tok16, tok16,
        pltpu.VMEM((chunks, 2 * rows, fc), BF16), pltpu.VMEM((rows, 1), F32),
        full16, full16, full32, full16, full16, full32, full16, full16,
        pltpu.VMEM((chunks, rows, fc), F32), pltpu.VMEM((chunks, rows, fc), BF16),
        pltpu.VMEM((chunks, rows, fc), BF16), pltpu.VMEM((rows, width), BF16),
        pltpu.VMEM((2 * rows, 2 * k), F32), tok16, tok16, small, small,
        dma((6,)), dma((3 * chunks + 3,)),
        dma((2,)), dma((2,)),
    ] + [dma((chunks,))] * 10 + [dma((2,)), dma((2,)), dma((1,)), dma((1,))]
    return pl.pallas_call(
        functools.partial(kernel, dist, chunks),
        out_shape=shapes,
        in_specs=[smem] + [any_space] * 5,
        out_specs=[any_space, smem] + [any_space] * 4,
        scratch_shapes=scratch,
        compiler_params=pltpu.CompilerParams(
            collective_id=level, has_side_effects=True, vmem_limit_bytes=48 * 1024 * 1024
        ),
        cost_estimate=pl.CostEstimate(flops=12 * rows * width * 2 * k, bytes_accessed=12_000_000, transcendentals=0),
    )(*operands)


def local(hidden, cotangent, numerator, push_weight, moment_one, moment_two, gossip_round):
    operands = (push_weight, hidden, cotangent, numerator, moment_one, moment_two)
    branches = [
        (lambda items, level=level: tuple(step_of(2**level, level, CHUNKS, items))) for level in range(ROUNDS)
    ]
    return lax.switch(gossip_round[0], branches, operands)


def solution(mesh):
    placed = (
        P(("rep", "tp"), None),
        P("rep", "tp"),
        P("rep", None, "tp"),
        P("rep"),
        P("rep", None, "tp"),
        P("rep", None, "tp"),
        P(),
    )
    return jax.shard_map(
        local,
        mesh=mesh,
        in_specs=placed,
        out_specs=(
            P("rep", None, "tp"),
            P("rep"),
            P("rep", None, "tp"),
            P("rep", None, "tp"),
            P("rep", "tp"),
            P(("rep", "tp"), None),
        ),
        check_vma=False,
    )
```

profile of v0, /device:TPU:0, one launch (start us, length us, event | category | flops | bytes accessed | tf_op | source)
XLA Modules:
  0.0 53.8 jit_solution(16021904516450121655)
XLA Ops:
  1.3 45.0 %conditional.1 = ((f32[1,2560,128]{2,1,0:T(8,128)S(1)}, f32[1]{0:T(128)}, f32[1,2560,128]{2,1,0:T(8,128)S(1)}, f32[1,2560,128]{2,1,0:T(8,128)}, bf16[1024,128]{1...) conditional(s32[]{:T(128)} %bitcast, (f32[1]{0:T(128)}, bf16[256,2560]{1,0:T(8,128)(2,1)}, ...), branch_computations={%region_0.0_spmd, %region_1.0_spmd, %region_2.0_spmd} | conditional | flops 2013265920 | bytes 12000008 | solution.py:268
  1.5 44.3 %branch_1_fun.1 = (f32[1,2560,128]{2,1,0:T(8,128)S(1)}, f32[1]{0:T(128)}, f32[1,2560,128]{2,1,0:T(8,128)S(1)}, f32[1,2560,128]{2,1,0:T(8,128)}, bf16[1024,128]{1...) custom-call(f32[1]{0:T(128)} %get-tuple-element.42.w_ref, bf16[256,2560]{1,0:T(8,128)(2,1)} %get-tuple-element.43.hid_hbm, ...), custom_call_target="tpu_custom_call" | custom-call | flops 2013265920 | bytes 12000000 | tf_op jit(solution)/shard_map/cond/branch_1_fun/pallas_call | solution.py:250
  46.2 1.1 %copy.55 = f32[1,2560,128]{2,1,0:T(8,128)} copy(f32[1,2560,128]{2,1,0:T(8,128)S(1)} %get-tuple-element.108) | data formatting | bytes 2621440
  48.0 0.0 copy-start
  48.0 1.1 %copy.57 = f32[1,2560,128]{2,1,0:T(8,128)} copy(f32[1,2560,128]{2,1,0:T(8,128)S(1)} %get-tuple-element.110) | data formatting | bytes 2621440
  49.1 0.7 %copy-done = f32[1,2560,128]{2,1,0:T(8,128)S(1)} copy-done((f32[1,2560,128]{2,1,0:T(8,128)S(1)}, f32[1,2560,128]{2,1,0:T(8,128)}, u32[]{:S(2)}) %copy-start) | copy-done | bytes 1310744
  49.8 0.0 copy-start.1
  49.8 1.1 %copy.58 = f32[1,2560,128]{2,1,0:T(8,128)} copy(f32[1,2560,128]{2,1,0:T(8,128)S(1)} %copy-done) | data formatting | bytes 2621440
  50.8 0.7 %copy.59 = bf16[1024,128]{1,0:T(8,128)(2,1)} copy(bf16[1024,128]{1,0:T(8,128)(2,1)S(1)} %get-tuple-element.112) | data formatting | bytes 524288
  51.5 0.0 copy-done.1
  51.6 1.1 %copy.60 = bf16[256,2560]{1,0:T(8,128)(2,1)} copy(bf16[256,2560]{1,0:T(8,128)(2,1)S(1)} %copy-done.1) | data formatting | bytes 2621440
Async XLA Ops:
  48.0 1.8 %copy-start = (f32[1,2560,128]{2,1,0:T(8,128)S(1)}, f32[1,2560,128]{2,1,0:T(8,128)}, u32[]{:S(2)}) copy-start(f32[1,2560,128]{2,1,0:T(8,128)} %get-tuple-element.111) | copy-start | bytes 3932164
  49.8 1.8 %copy-start.1 = (bf16[256,2560]{1,0:T(8,128)(2,1)S(1)}, bf16[256,2560]{1,0:T(8,128)(2,1)}, u32[]{:S(2)}) copy-start(bf16[256,2560]{1,0:T(8,128)(2,1)} %get-tuple-element.113) | copy-start | bytes 3932164
where the time goes:
time: 54.6 us; the launch traced here: 53.8 us
  Pallas kernels  44.3 us (81%)
  local copies, waits for them, and re-layouts  5.68 us (10%)
  between operations  3.12 us (6%)
  loops' own time  0.69 us (1%)
    pallas_call x1, Pallas kernels, step_of(): pl.pallas_call(functools.partial(kernel, dist, chunks), out_shape=shapes,...  44.3 us
    unnamed x9, local copies, waits for them, and re-layouts  5.68 us

commit v1 on v0

--- a/solution.py
+++ b/solution.py
@@ -11,8 +11,8 @@
 F32 = jnp.float32
 BF16 = jnp.bfloat16
 ROUNDS = 3
-CHUNKS = 5
-EARLY = 1
+CHUNKS = 10
+EARLY = 2
 
 
 def kernel(
@@ -39,9 +39,12 @@
     def row_block(index):
         return pl.ds(pl.multiple_of(index * rows, rows), rows)
 
+    barrier = pltpu.get_barrier_semaphore()
+    for device in (near_dev, far_dev, to_dev, from_dev):
+        pl.semaphore_signal(barrier, inc=1, device_id=device, device_id_type=MESH)
     loads = [
+        pltpu.make_async_copy(num_hbm.at[0], num, load_sem.at[1]),
         pltpu.make_async_copy(hid_hbm, hid, load_sem.at[0]),
-        pltpu.make_async_copy(num_hbm.at[0], num, load_sem.at[1]),
         pltpu.make_async_copy(cot_hbm.at[row_block(tp)], cot_own.at[pl.ds(0, rows)], load_sem.at[2]),
         pltpu.make_async_copy(cot_hbm.at[row_block(near)], cot_own.at[pl.ds(rows, rows)], load_sem.at[3]),
         pltpu.make_async_copy(m1_hbm.at[0], m1, load_sem.at[4]),
@@ -49,10 +52,12 @@
     ]
     for load in loads:
         load.start()
-
-    barrier = pltpu.get_barrier_semaphore()
-    for device in (near_dev, far_dev, to_dev, from_dev):
-        pl.semaphore_signal(barrier, inc=1, device_id=device, device_id_type=MESH)
+    weight = w_ref[0]
+    w_send[...] = jnp.full(w_send.shape, weight, F32)
+    part = [pl.ds(c * fc, fc) for c in range(chunks)]
+    loads[0].wait()
+    for here in part:
+        deb_own[here, :] = (num[here, :] / jnp.full((1, 1), weight, F32)).astype(BF16)
     pl.semaphore_wait(barrier, 4)
 
     def remote(src, dst, send, recv, device):
@@ -66,7 +71,6 @@
     ]
     for copy in cot_copies:
         copy.start()
-    part = [pl.ds(c * fc, fc) for c in range(chunks)]
     nrm_copies = [
         remote(nrm.at[c, pl.ds(0, rows)], nrm.at[c, pl.ds(rows, rows)], nrm_s.at[c], nrm_r.at[c], near_dev)
         for c in range(chunks)
@@ -88,12 +92,12 @@
         remote(val_send.at[pl.ds(0, rows)], val_hbm.at[row_block(tp)], val_s.at[0], val_r.at[0], far_dev),
         remote(val_send.at[pl.ds(rows, rows)], val_hbm.at[row_block(near)], val_s.at[1], val_r.at[1], far_dev),
     ]
-    weight = w_ref[0]
-    w_send[...] = jnp.full(w_send.shape, weight, F32)
+    for copy in deb_copies[:EARLY]:
+        copy.start()
     w_copy = remote(w_send, w_far, w_s.at[0], w_r.at[0], to_dev)
     w_copy.start()
 
-    loads[0].wait()
+    loads[1].wait()
     step = 32
 
     @pl.loop(0, rows // step)
@@ -108,15 +112,6 @@
 
     for copy in nrm_copies:
         copy.start()
-
-    loads[1].wait()
-
-    def send_deb(c):
-        deb_own[part[c], :] = (num[part[c], :] / jnp.full((1, 1), weight, F32)).astype(BF16)
-        deb_copies[c].start()
-
-    for c in range(EARLY):
-        send_deb(c)
 
     loads[2].wait()
     loads[3].wait()
@@ -130,8 +125,8 @@
         g_send[part[c], :] = p[:, k:].astype(BF16)
         g_copies[c].start()
         g_own[part[c], :] = p[:, :k]
-    for c in range(EARLY, chunks):
-        send_deb(c)
+    for copy in deb_copies[EARLY:]:
+        copy.start()
 
     loads[4].wait()
     loads[5].wait()
@@ -187,6 +182,15 @@
     for c in range(chunks):
         forward(c)
 
+    def mix(c):
+        half_copies[c].wait_recv()
+        here = part[c]
+        num[here, :] = 0.5 * (half[here, :] + half_far[here, :].astype(F32))
+        write(num.at[here], numo_hbm.at[0, here])
+
+    lead = chunks // 2
+    for c in range(lead):
+        mix(c)
     inner = jnp.zeros((rows, 1), F32)
     for c in range(chunks):
         gn_copies[c].wait_recv()
@@ -195,17 +199,17 @@
         normal = hid[:, c * fc:(c + 1) * fc].astype(F32) * scale[...]
         inner = inner + jnp.sum(total * normal, axis=1, keepdims=True)
     inner = inner / width
-    for c in range(chunks):
-        s = scale[...]
-        normal = hid[:, c * fc:(c + 1) * fc].astype(F32) * s
-        gh[:, c * fc:(c + 1) * fc] = (s * (gn[c] - normal * inner)).astype(BF16)
-    write(gh, gh_hbm)
-
-    for c in range(chunks):
-        half_copies[c].wait_recv()
-        here = part[c]
-        num[here, :] = 0.5 * (half[here, :] + half_far[here, :].astype(F32))
-        write(num.at[here], numo_hbm.at[0, here])
+    quarter = rows // 4
+    for q in range(4):
+        some = pl.ds(q * quarter, quarter)
+        s = scale[some, :]
+        mean = inner[q * quarter:(q + 1) * quarter]
+        for c in range(chunks):
+            normal = hid[some, c * fc:(c + 1) * fc].astype(F32) * s
+            gh[some, c * fc:(c + 1) * fc] = (s * (gn[c, some, :] - normal * mean)).astype(BF16)
+        write(gh.at[some], gh_hbm.at[some])
+    for c in range(lead, chunks):
+        mix(c)
     w_copy.wait_recv()
     wo_ref[0] = 0.5 * (weight + jnp.max(w_far[...]))
 
@@ -244,7 +248,7 @@
         pltpu.VMEM((chunks, rows, fc), F32), pltpu.VMEM((chunks, rows, fc), BF16),
         pltpu.VMEM((chunks, rows, fc), BF16), pltpu.VMEM((rows, width), BF16),
         pltpu.VMEM((2 * rows, 2 * k), F32), tok16, tok16, small, small,
-        dma((6,)), dma((3 * chunks + 3,)),
+        dma((6,)), dma((3 * chunks + 6,)),
         dma((2,)), dma((2,)),
     ] + [dma((chunks,))] * 10 + [dma((2,)), dma((2,)), dma((1,)), dma((1,))]
     return pl.pallas_call(
@@ -260,12 +264,41 @@
     )(*operands)
 
 
+def place_kernel(pieces, count, *refs):
+    sources, targets, sem = refs[:count], refs[count:2 * count], refs[2 * count]
+    copies = []
+    for source, target in zip(sources, targets):
+        size = source.shape[-2] // pieces
+        for piece in range(pieces):
+            some = pl.ds(piece * size, size)
+            at = (0, some) if len(source.shape) == 3 else (some,)
+            copies.append(pltpu.make_async_copy(source.at[at], target.at[at], sem.at[len(copies)]))
+            copies[-1].start()
+    for copy in copies:
+        copy.wait()
+
+
+def place(arrays, pieces=4):
+    count = len(arrays)
+    any_space = pl.BlockSpec(memory_space=pl.ANY)
+    return pl.pallas_call(
+        functools.partial(place_kernel, pieces, count),
+        out_shape=[jax.ShapeDtypeStruct(a.shape, a.dtype) for a in arrays],
+        in_specs=[any_space] * count,
+        out_specs=[any_space] * count,
+        scratch_shapes=[pltpu.SemaphoreType.DMA((pieces * count,))],
+        compiler_params=pltpu.CompilerParams(vmem_limit_bytes=1024 * 1024),
+    )(*arrays)
+
+
 def local(hidden, cotangent, numerator, push_weight, moment_one, moment_two, gossip_round):
     operands = (push_weight, hidden, cotangent, numerator, moment_one, moment_two)
     branches = [
         (lambda items, level=level: tuple(step_of(2**level, level, CHUNKS, items))) for level in range(ROUNDS)
     ]
-    return lax.switch(gossip_round[0], branches, operands)
+    numerator_out, weight_out, *others = lax.switch(gossip_round[0], branches, operands)
+    numerator_out, first, second, values, grad_hidden = place([numerator_out, *others])
+    return numerator_out, weight_out, first, second, values, grad_hidden
 
 
 def solution(mesh):

time: 54.6 us -> 131 us (2.40)
  Pallas kernels: 44.3 us -> 127 us
  local copies, waits for them, and re-layouts: 5.68 us -> 0 us
    pallas_call x0 -> x1, Pallas kernels: none -> 80.7 us  [place(): pl.pallas_call(functools.partial(place_kernel, pieces, count), out_shape=...]
    unnamed x9 -> x0, local copies, waits for them, and re-layouts: 5.68 us -> none
    pallas_call x1, Pallas kernels: 44.3 us -> 46.5 us  [step_of(): pl.pallas_call(functools.partial(kernel, dist, chunks), out_shape=shapes,...]
where the time goes in v1:
time: 131 us
  Pallas kernels  127 us (97%)
  between operations  3.11 us (2%)
    pallas_call x1, Pallas kernels, place(): pl.pallas_call(functools.partial(place_kernel, pieces, count), out_shape=...  80.7 us
    pallas_call x1, Pallas kernels, step_of(): pl.pallas_call(functools.partial(kernel, dist, chunks), out_shape=shapes,...  46.5 us

profile of v1, /device:TPU:0, one launch (start us, length us, event | category | flops | bytes accessed | tf_op | source)
XLA Modules:
  0.0 131.0 jit_solution(10108463960417214143)
XLA Ops:
  1.3 47.2 %conditional.1 = ((f32[1,2560,128]{2,1,0:T(8,128)S(1)}, f32[1]{0:T(128)}, f32[1,2560,128]{2,1,0:T(8,128)S(1)}, f32[1,2560,128]{2,1,0:T(8,128)}, bf16[1024,128]{1...) conditional(s32[]{:T(128)} %bitcast, (f32[1]{0:T(128)}, bf16[256,2560]{1,0:T(8,128)(2,1)}, ...), branch_computations={%region_0.0_spmd, %region_1.0_spmd, %region_2.0_spmd} | conditional | flops 2013265920 | bytes 12000008 | solution.py:299
  1.7 46.5 %branch_2_fun.1 = (f32[1,2560,128]{2,1,0:T(8,128)S(1)}, f32[1]{0:T(128)}, f32[1,2560,128]{2,1,0:T(8,128)S(1)}, f32[1,2560,128]{2,1,0:T(8,128)}, bf16[1024,128]{1...) custom-call(f32[1]{0:T(128)} %get-tuple-element.48.w_ref, bf16[256,2560]{1,0:T(8,128)(2,1)} %get-tuple-element.49.hid_hbm, ...), custom_call_target="tpu_custom_call" | custom-call | flops 2013265920 | bytes 12000000 | tf_op jit(solution)/shard_map/cond/branch_2_fun/pallas_call | solution.py:254
  48.5 80.7 %shard_map.118 = (f32[1,2560,128]{2,1,0:T(8,128)}, f32[1,2560,128]{2,1,0:T(8,128)}, f32[1,2560,128]{2,1,0:T(8,128)}, bf16[1024,128]{1,0:T(8,128)(2,1)}, bf16[256,2560]{1,0:T(8,128)(2,1)}) custom-call(f32[1,2560,128]{2,1,0:T(8,128)S(1)} %get-tuple-element.71.refs_0_, f32[1,2560,128]{2,1,0:T(8,128)S(1)} %get-tuple-element.72.refs_1_, ...), custom_call_target="tpu_custom_call" | custom-call | tf_op jit(solution)/shard_map/pallas_call | solution.py:284

commit v2 on v1

--- a/solution.py
+++ b/solution.py
@@ -11,8 +11,7 @@
 F32 = jnp.float32
 BF16 = jnp.bfloat16
 ROUNDS = 3
-CHUNKS = 10
-EARLY = 2
+CHUNKS = 5
 
 
 def kernel(
@@ -43,8 +42,8 @@
     for device in (near_dev, far_dev, to_dev, from_dev):
         pl.semaphore_signal(barrier, inc=1, device_id=device, device_id_type=MESH)
     loads = [
+        pltpu.make_async_copy(hid_hbm, hid, load_sem.at[0]),
         pltpu.make_async_copy(num_hbm.at[0], num, load_sem.at[1]),
-        pltpu.make_async_copy(hid_hbm, hid, load_sem.at[0]),
         pltpu.make_async_copy(cot_hbm.at[row_block(tp)], cot_own.at[pl.ds(0, rows)], load_sem.at[2]),
         pltpu.make_async_copy(cot_hbm.at[row_block(near)], cot_own.at[pl.ds(rows, rows)], load_sem.at[3]),
         pltpu.make_async_copy(m1_hbm.at[0], m1, load_sem.at[4]),
@@ -55,9 +54,6 @@
     weight = w_ref[0]
     w_send[...] = jnp.full(w_send.shape, weight, F32)
     part = [pl.ds(c * fc, fc) for c in range(chunks)]
-    loads[0].wait()
-    for here in part:
-        deb_own[here, :] = (num[here, :] / jnp.full((1, 1), weight, F32)).astype(BF16)
     pl.semaphore_wait(barrier, 4)
 
     def remote(src, dst, send, recv, device):
@@ -92,12 +88,10 @@
         remote(val_send.at[pl.ds(0, rows)], val_hbm.at[row_block(tp)], val_s.at[0], val_r.at[0], far_dev),
         remote(val_send.at[pl.ds(rows, rows)], val_hbm.at[row_block(near)], val_s.at[1], val_r.at[1], far_dev),
     ]
-    for copy in deb_copies[:EARLY]:
-        copy.start()
     w_copy = remote(w_send, w_far, w_s.at[0], w_r.at[0], to_dev)
     w_copy.start()
 
-    loads[1].wait()
+    loads[0].wait()
     step = 32
 
     @pl.loop(0, rows // step)
@@ -113,6 +107,13 @@
     for copy in nrm_copies:
         copy.start()
 
+    loads[1].wait()
+
+    def send_deb(c):
+        deb_own[part[c], :] = (num[part[c], :] / jnp.full((1, 1), weight, F32)).astype(BF16)
+        deb_copies[c].start()
+
+    send_deb(0)
     loads[2].wait()
     loads[3].wait()
     for copy in cot_copies:
@@ -124,9 +125,9 @@
         p = lax.dot_general(nrm[c], cot2, (((0,), (0,)), ((), ())), preferred_element_type=F32)
         g_send[part[c], :] = p[:, k:].astype(BF16)
         g_copies[c].start()
+        if c < chunks - 1:
+            send_deb(c + 1)
         g_own[part[c], :] = p[:, :k]
-    for copy in deb_copies[EARLY:]:
-        copy.start()
 
     loads[4].wait()
     loads[5].wait()
@@ -177,10 +178,11 @@
         both = jnp.concatenate([cot_own[pl.ds(0, rows), :], cot_far[pl.ds(0, rows), :]], axis=1)
         gn[c] = lax.dot_general(both, deb2, dims, preferred_element_type=F32)
 
-    for c in range(chunks):
+    for c in range(chunks - 1):
         moments(c)
-    for c in range(chunks):
         forward(c)
+    forward(chunks - 1)
+    moments(chunks - 1)
 
     def mix(c):
         half_copies[c].wait_recv()
@@ -265,29 +267,39 @@
 
 
 def place_kernel(pieces, count, *refs):
-    sources, targets, sem = refs[:count], refs[count:2 * count], refs[2 * count]
-    copies = []
-    for source, target in zip(sources, targets):
+    sources, targets, stages = refs[:count], refs[count:2 * count], refs[2 * count:3 * count]
+    in_sem, out_sem = refs[3 * count:]
+    steps = []
+    for source, stage, target in zip(sources, stages, targets):
         size = source.shape[-2] // pieces
         for piece in range(pieces):
             some = pl.ds(piece * size, size)
             at = (0, some) if len(source.shape) == 3 else (some,)
-            copies.append(pltpu.make_async_copy(source.at[at], target.at[at], sem.at[len(copies)]))
-            copies[-1].start()
-    for copy in copies:
-        copy.wait()
-
-
-def place(arrays, pieces=4):
+            index = len(steps)
+            steps.append((
+                pltpu.make_async_copy(source.at[at], stage.at[at], in_sem.at[index]),
+                pltpu.make_async_copy(stage.at[at], target.at[at], out_sem.at[index]),
+            ))
+    for arrive, _ in steps:
+        arrive.start()
+    for arrive, leave in steps:
+        arrive.wait()
+        leave.start()
+    for _, leave in steps:
+        leave.wait()
+
+
+def place(arrays, pieces=2):
     count = len(arrays)
     any_space = pl.BlockSpec(memory_space=pl.ANY)
+    sems = pltpu.SemaphoreType.DMA((pieces * count,))
     return pl.pallas_call(
         functools.partial(place_kernel, pieces, count),
         out_shape=[jax.ShapeDtypeStruct(a.shape, a.dtype) for a in arrays],
         in_specs=[any_space] * count,
         out_specs=[any_space] * count,
-        scratch_shapes=[pltpu.SemaphoreType.DMA((pieces * count,))],
-        compiler_params=pltpu.CompilerParams(vmem_limit_bytes=1024 * 1024),
+        scratch_shapes=[pltpu.VMEM(a.shape, a.dtype) for a in arrays] + [sems, sems],
+        compiler_params=pltpu.CompilerParams(vmem_limit_bytes=16 * 1024 * 1024),
     )(*arrays)
 
 

time: 131 us -> 54.4 us (0.42)
  Pallas kernels: 127 us -> 51 us
    pallas_call x1, Pallas kernels: 80.7 us -> 4.66 us  [place(): pl.pallas_call(functools.partial(place_kernel, pieces, count), out_shape=...]
where the time goes in v2:
time: 54.4 us
  Pallas kernels  51 us (94%)
  between operations  3.11 us (6%)
    pallas_call x1, Pallas kernels, step_of(): pl.pallas_call(functools.partial(kernel, dist, chunks), out_shape=shapes,...  46.4 us
    pallas_call x1, Pallas kernels, place(): pl.pallas_call(functools.partial(place_kernel, pieces, count), out_shape=...  4.66 us

profile of v2, /device:TPU:0, one launch (start us, length us, event | category | flops | bytes accessed | tf_op | source)
XLA Modules:
  0.0 54.4 jit_solution(18288710683586327336)
XLA Ops:
  1.3 46.7 %conditional.1 = ((f32[1,2560,128]{2,1,0:T(8,128)S(1)}, f32[1]{0:T(128)}, f32[1,2560,128]{2,1,0:T(8,128)S(1)}, f32[1,2560,128]{2,1,0:T(8,128)}, bf16[1024,128]{1...) conditional(s32[]{:T(128)} %bitcast, (f32[1]{0:T(128)}, bf16[256,2560]{1,0:T(8,128)(2,1)}, ...), branch_computations={%region_0.0_spmd, %region_1.0_spmd, %region_2.0_spmd} | conditional | flops 2013265920 | bytes 12000008 | solution.py:311
  1.3 46.4 %branch_0_fun.1 = (f32[1,2560,128]{2,1,0:T(8,128)S(1)}, f32[1]{0:T(128)}, f32[1,2560,128]{2,1,0:T(8,128)S(1)}, f32[1,2560,128]{2,1,0:T(8,128)}, bf16[1024,128]{1...) custom-call(f32[1]{0:T(128)} %get-tuple-element.36.w_ref, bf16[256,2560]{1,0:T(8,128)(2,1)} %get-tuple-element.37.hid_hbm, ...), custom_call_target="tpu_custom_call" | custom-call | flops 2013265920 | bytes 12000000 | tf_op jit(solution)/shard_map/cond/branch_0_fun/pallas_call | solution.py:256
  48.0 4.7 %shard_map.118 = (f32[1,2560,128]{2,1,0:T(8,128)}, f32[1,2560,128]{2,1,0:T(8,128)}, f32[1,2560,128]{2,1,0:T(8,128)}, bf16[1024,128]{1,0:T(8,128)(2,1)}, bf16[256,2560]{1,0:T(8,128)(2,1)}) custom-call(f32[1,2560,128]{2,1,0:T(8,128)S(1)} %get-tuple-element.71.refs_0_, f32[1,2560,128]{2,1,0:T(8,128)S(1)} %get-tuple-element.72.refs_1_, ...), custom_call_target="tpu_custom_call" | custom-call | tf_op jit(solution)/shard_map/pallas_call | solution.py:296

commit v3 on v1

--- a/solution.py
+++ b/solution.py
@@ -12,7 +12,7 @@
 BF16 = jnp.bfloat16
 ROUNDS = 3
 CHUNKS = 10
-EARLY = 2
+EARLY = 3
 
 
 def kernel(
@@ -43,21 +43,18 @@
     for device in (near_dev, far_dev, to_dev, from_dev):
         pl.semaphore_signal(barrier, inc=1, device_id=device, device_id_type=MESH)
     loads = [
-        pltpu.make_async_copy(num_hbm.at[0], num, load_sem.at[1]),
-        pltpu.make_async_copy(hid_hbm, hid, load_sem.at[0]),
+        pltpu.make_async_copy(num_hbm.at[0], num, load_sem.at[0]),
+        pltpu.make_async_copy(hid_hbm, hid, load_sem.at[1]),
         pltpu.make_async_copy(cot_hbm.at[row_block(tp)], cot_own.at[pl.ds(0, rows)], load_sem.at[2]),
         pltpu.make_async_copy(cot_hbm.at[row_block(near)], cot_own.at[pl.ds(rows, rows)], load_sem.at[3]),
         pltpu.make_async_copy(m1_hbm.at[0], m1, load_sem.at[4]),
         pltpu.make_async_copy(m2_hbm.at[0], m2, load_sem.at[5]),
     ]
-    for load in loads:
+    for load in loads[:4]:
         load.start()
     weight = w_ref[0]
     w_send[...] = jnp.full(w_send.shape, weight, F32)
     part = [pl.ds(c * fc, fc) for c in range(chunks)]
-    loads[0].wait()
-    for here in part:
-        deb_own[here, :] = (num[here, :] / jnp.full((1, 1), weight, F32)).astype(BF16)
     pl.semaphore_wait(barrier, 4)
 
     def remote(src, dst, send, recv, device):
@@ -92,11 +89,16 @@
         remote(val_send.at[pl.ds(0, rows)], val_hbm.at[row_block(tp)], val_s.at[0], val_r.at[0], far_dev),
         remote(val_send.at[pl.ds(rows, rows)], val_hbm.at[row_block(near)], val_s.at[1], val_r.at[1], far_dev),
     ]
-    for copy in deb_copies[:EARLY]:
-        copy.start()
     w_copy = remote(w_send, w_far, w_s.at[0], w_r.at[0], to_dev)
     w_copy.start()
 
+    def send_deb(c):
+        deb_own[part[c], :] = (num[part[c], :] / jnp.full((1, 1), weight, F32)).astype(BF16)
+        deb_copies[c].start()
+
+    loads[0].wait()
+    for c in range(EARLY):
+        send_deb(c)
     loads[1].wait()
     step = 32
 
@@ -113,6 +115,8 @@
     for copy in nrm_copies:
         copy.start()
 
+    for load in loads[4:]:
+        load.start()
     loads[2].wait()
     loads[3].wait()
     for copy in cot_copies:
@@ -125,8 +129,8 @@
         g_send[part[c], :] = p[:, k:].astype(BF16)
         g_copies[c].start()
         g_own[part[c], :] = p[:, :k]
-    for copy in deb_copies[EARLY:]:
-        copy.start()
+    for c in range(EARLY, chunks):
+        send_deb(c)
 
     loads[4].wait()
     loads[5].wait()
@@ -154,14 +158,20 @@
         write(m1.at[here], m1o_hbm.at[0, here])
         write(m2.at[here], m2o_hbm.at[0, here])
 
+    def swap_grad_normed(c, deb2):
+        dims = (((1,), (1,)), ((), ()))
+        both = jnp.concatenate([cot_own[pl.ds(rows, rows), :], cot_far[pl.ds(rows, rows), :]], axis=1)
+        gn_send[c] = lax.dot_general(both, deb2, dims, preferred_element_type=F32).astype(BF16)
+        gn_copies[c].start()
+        both = jnp.concatenate([cot_own[pl.ds(0, rows), :], cot_far[pl.ds(0, rows), :]], axis=1)
+        gn[c] = lax.dot_general(both, deb2, dims, preferred_element_type=F32)
+
     def forward(c):
         deb_copies[c].wait_recv()
         here = part[c]
         deb2 = jnp.concatenate([deb_own[here, :], deb_far[here, :]], axis=1)
-        dims = (((1,), (1,)), ((), ()))
-        both = jnp.concatenate([cot_own[pl.ds(rows, rows), :], cot_far[pl.ds(rows, rows), :]], axis=1)
-        gn_send[c] = lax.dot_general(both, deb2, dims, preferred_element_type=F32).astype(BF16)
-        gn_copies[c].start()
+        if c < chunks - 1:
+            swap_grad_normed(c, deb2)
         product = jnp.dot(nrm[c], deb2, preferred_element_type=F32)
         if c:
             product = val_acc[...] + product
@@ -171,16 +181,17 @@
             val_send[...] = product[:, k:].astype(BF16)
             for copy in val_copies:
                 copy.start()
+            swap_grad_normed(c, deb2)
             val_own[...] = product[:, :k].astype(BF16)
             write(val_own.at[pl.ds(0, rows)], val_hbm.at[row_block(tp)])
             write(val_own.at[pl.ds(rows, rows)], val_hbm.at[row_block(near)])
-        both = jnp.concatenate([cot_own[pl.ds(0, rows), :], cot_far[pl.ds(0, rows), :]], axis=1)
-        gn[c] = lax.dot_general(both, deb2, dims, preferred_element_type=F32)
-
-    for c in range(chunks):
-        moments(c)
-    for c in range(chunks):
-        forward(c)
+
+    def add_inner(c, inner):
+        gn_copies[c].wait_recv()
+        total = gn[c] + gn_near[c].astype(F32)
+        gn[c] = total
+        normal = hid[:, c * fc:(c + 1) * fc].astype(F32) * scale[...]
+        return inner + jnp.sum(total * normal, axis=1, keepdims=True)
 
     def mix(c):
         half_copies[c].wait_recv()
@@ -188,17 +199,19 @@
         num[here, :] = 0.5 * (half[here, :] + half_far[here, :].astype(F32))
         write(num.at[here], numo_hbm.at[0, here])
 
-    lead = chunks // 2
-    for c in range(lead):
-        mix(c)
+    for c in range(chunks):
+        moments(c)
     inner = jnp.zeros((rows, 1), F32)
+    mixed = 0
     for c in range(chunks):
-        gn_copies[c].wait_recv()
-        total = gn[c] + gn_near[c].astype(F32)
-        gn[c] = total
-        normal = hid[:, c * fc:(c + 1) * fc].astype(F32) * scale[...]
-        inner = inner + jnp.sum(total * normal, axis=1, keepdims=True)
-    inner = inner / width
+        forward(c)
+        if c:
+            inner = add_inner(c - 1, inner)
+        ready = c if dist < 4 else c // 2
+        while mixed < ready:
+            mix(mixed)
+            mixed += 1
+    inner = add_inner(chunks - 1, inner) / width
     quarter = rows // 4
     for q in range(4):
         some = pl.ds(q * quarter, quarter)
@@ -208,7 +221,7 @@
             normal = hid[some, c * fc:(c + 1) * fc].astype(F32) * s
             gh[some, c * fc:(c + 1) * fc] = (s * (gn[c, some, :] - normal * mean)).astype(BF16)
         write(gh.at[some], gh_hbm.at[some])
-    for c in range(lead, chunks):
+    for c in range(mixed, chunks):
         mix(c)
     w_copy.wait_recv()
     wo_ref[0] = 0.5 * (weight + jnp.max(w_far[...]))
@@ -258,7 +271,7 @@
         out_specs=[any_space, smem] + [any_space] * 4,
         scratch_shapes=scratch,
         compiler_params=pltpu.CompilerParams(
-            collective_id=level, has_side_effects=True, vmem_limit_bytes=48 * 1024 * 1024
+            collective_id=level, has_side_effects=True, vmem_limit_bytes=28 * 1024 * 1024
         ),
         cost_estimate=pl.CostEstimate(flops=12 * rows * width * 2 * k, bytes_accessed=12_000_000, transcendentals=0),
     )(*operands)
@@ -278,16 +291,15 @@
         copy.wait()
 
 
-def place(arrays, pieces=4):
+def place(arrays, pieces=2):
     count = len(arrays)
-    any_space = pl.BlockSpec(memory_space=pl.ANY)
     return pl.pallas_call(
         functools.partial(place_kernel, pieces, count),
         out_shape=[jax.ShapeDtypeStruct(a.shape, a.dtype) for a in arrays],
-        in_specs=[any_space] * count,
-        out_specs=[any_space] * count,
+        in_specs=[pl.BlockSpec(memory_space=pltpu.VMEM)] * count,
+        out_specs=[pl.BlockSpec(memory_space=pl.ANY)] * count,
         scratch_shapes=[pltpu.SemaphoreType.DMA((pieces * count,))],
-        compiler_params=pltpu.CompilerParams(vmem_limit_bytes=1024 * 1024),
+        compiler_params=pltpu.CompilerParams(vmem_limit_bytes=16 * 1024 * 1024),
     )(*arrays)
 
 

time: 131 us -> 54.3 us (0.41)
  Pallas kernels: 127 us -> 50.7 us
    pallas_call x1, Pallas kernels: 80.7 us -> 4.21 us  [place(): pl.pallas_call(functools.partial(place_kernel, pieces, count), out_shape=...]
where the time goes in v3:
time: 54.3 us; the launch traced here: 54.1 us
  Pallas kernels  50.7 us (93%)
  between operations  3.11 us (6%)
    pallas_call x1, Pallas kernels, step_of(): pl.pallas_call(functools.partial(kernel, dist, chunks), out_shape=shapes,...  46.5 us
    pallas_call x1, Pallas kernels, place(): pl.pallas_call(functools.partial(place_kernel, pieces, count), out_shape=...  4.21 us

profile of v3, /device:TPU:0, one launch (start us, length us, event | category | flops | bytes accessed | tf_op | source)
XLA Modules:
  0.0 54.1 jit_solution(11123292304121356229)
XLA Ops:
  1.3 46.8 %conditional.1 = ((f32[1,2560,128]{2,1,0:T(8,128)S(1)}, f32[1]{0:T(128)}, f32[1,2560,128]{2,1,0:T(8,128)S(1)}, f32[1,2560,128]{2,1,0:T(8,128)}, bf16[1024,128]{1...) conditional(s32[]{:T(128)} %bitcast, (f32[1]{0:T(128)}, bf16[256,2560]{1,0:T(8,128)(2,1)}, ...), branch_computations={%region_0.0_spmd, %region_1.0_spmd, %region_2.0_spmd} | conditional | flops 2013265920 | bytes 12000008 | solution.py:311
  1.3 46.5 %branch_0_fun.1 = (f32[1,2560,128]{2,1,0:T(8,128)S(1)}, f32[1]{0:T(128)}, f32[1,2560,128]{2,1,0:T(8,128)S(1)}, f32[1,2560,128]{2,1,0:T(8,128)}, bf16[1024,128]{1...) custom-call(f32[1]{0:T(128)} %get-tuple-element.36.w_ref, bf16[256,2560]{1,0:T(8,128)(2,1)} %get-tuple-element.37.hid_hbm, ...), custom_call_target="tpu_custom_call" | custom-call | flops 2013265920 | bytes 12000000 | tf_op jit(solution)/shard_map/cond/branch_0_fun/pallas_call | solution.py:267
  48.1 4.2 %shard_map.118 = (f32[1,2560,128]{2,1,0:T(8,128)}, f32[1,2560,128]{2,1,0:T(8,128)}, f32[1,2560,128]{2,1,0:T(8,128)}, bf16[1024,128]{1,0:T(8,128)(2,1)}, bf16[256,2560]{1,0:T(8,128)(2,1)}) custom-call(f32[1,2560,128]{2,1,0:T(8,128)S(1)} %get-tuple-element.71.refs_0_, f32[1,2560,128]{2,1,0:T(8,128)S(1)} %get-tuple-element.72.refs_1_, ...), custom_call_target="tpu_custom_call" | custom-call | tf_op jit(solution)/shard_map/pallas_call | solution.py:296

commit v4 on v3

--- a/solution.py
+++ b/solution.py
@@ -11,8 +11,8 @@
 F32 = jnp.float32
 BF16 = jnp.bfloat16
 ROUNDS = 3
-CHUNKS = 10
-EARLY = 3
+CHUNKS = 5
+EARLY = 1
 
 
 def kernel(
@@ -277,30 +277,43 @@
     )(*operands)
 
 
-def place_kernel(pieces, count, *refs):
-    sources, targets, sem = refs[:count], refs[count:2 * count], refs[2 * count]
-    copies = []
-    for source, target in zip(sources, targets):
-        size = source.shape[-2] // pieces
-        for piece in range(pieces):
-            some = pl.ds(piece * size, size)
-            at = (0, some) if len(source.shape) == 3 else (some,)
-            copies.append(pltpu.make_async_copy(source.at[at], target.at[at], sem.at[len(copies)]))
-            copies[-1].start()
-    for copy in copies:
+def place_kernel(held, count, weight_in, *refs):
+    sources, weight_out, targets = refs[:count], refs[count], refs[count + 1:2 * count + 1]
+    stages, (in_sem, out_sem) = refs[2 * count + 1:-2], refs[-2:]
+    weight = pltpu.make_async_copy(weight_in, weight_out, out_sem.at[count])
+    weight.start()
+    arrivals = [
+        pltpu.make_async_copy(source, stage, in_sem.at[index])
+        for index, (source, stage) in enumerate(zip(sources[held:], stages))
+    ]
+    for arrival in arrivals:
+        arrival.start()
+    leaving = [
+        pltpu.make_async_copy(source, target, out_sem.at[index])
+        for index, (source, target) in enumerate(zip((*sources[:held], *stages), targets))
+    ]
+    for copy in leaving[:held]:
+        copy.start()
+    for arrival, copy in zip(arrivals, leaving[held:]):
+        arrival.wait()
+        copy.start()
+    for copy in (*leaving, weight):
         copy.wait()
 
 
-def place(arrays, pieces=2):
-    count = len(arrays)
+def place(weight, held, staged):
+    arrays = [*held, *staged]
+    any_space = pl.BlockSpec(memory_space=pl.ANY)
+    in_vmem = pl.BlockSpec(memory_space=pltpu.VMEM)
     return pl.pallas_call(
-        functools.partial(place_kernel, pieces, count),
-        out_shape=[jax.ShapeDtypeStruct(a.shape, a.dtype) for a in arrays],
-        in_specs=[pl.BlockSpec(memory_space=pltpu.VMEM)] * count,
-        out_specs=[pl.BlockSpec(memory_space=pl.ANY)] * count,
-        scratch_shapes=[pltpu.SemaphoreType.DMA((pieces * count,))],
+        functools.partial(place_kernel, len(held), len(arrays)),
+        out_shape=[jax.ShapeDtypeStruct(a.shape, a.dtype) for a in (weight, *arrays)],
+        in_specs=[any_space] + [in_vmem] * len(held) + [any_space] * len(staged),
+        out_specs=[any_space] * (1 + len(arrays)),
+        scratch_shapes=[pltpu.VMEM(a.shape, a.dtype) for a in staged]
+        + [pltpu.SemaphoreType.DMA((len(staged),)), pltpu.SemaphoreType.DMA((len(arrays) + 1,))],
         compiler_params=pltpu.CompilerParams(vmem_limit_bytes=16 * 1024 * 1024),
-    )(*arrays)
+    )(weight, *arrays)
 
 
 def local(hidden, cotangent, numerator, push_weight, moment_one, moment_two, gossip_round):
@@ -308,8 +321,10 @@
     branches = [
         (lambda items, level=level: tuple(step_of(2**level, level, CHUNKS, items))) for level in range(ROUNDS)
     ]
-    numerator_out, weight_out, *others = lax.switch(gossip_round[0], branches, operands)
-    numerator_out, first, second, values, grad_hidden = place([numerator_out, *others])
+    numerator_out, weight_out, first, second, values, grad_hidden = lax.switch(gossip_round[0], branches, operands)
+    weight_out, numerator_out, first, values, second, grad_hidden = place(
+        weight_out, [numerator_out, first, values], [second, grad_hidden]
+    )
     return numerator_out, weight_out, first, second, values, grad_hidden
 
 

time: 54.3 us -> 52 us (0.958)
  between operations: 3.11 us -> 1.49 us
  Pallas kernels: 50.7 us -> 49.5 us
    pallas_call x1, Pallas kernels: 46.5 us -> 45 us  [step_of(): pl.pallas_call(functools.partial(kernel, dist, chunks), out_shape=shapes,...]
where the time goes in v4:
time: 52 us; the launch traced here: 51.3 us
  Pallas kernels  49.5 us (95%)
  between operations  1.49 us (3%)
    pallas_call x1, Pallas kernels, step_of(): pl.pallas_call(functools.partial(kernel, dist, chunks), out_shape=shapes,...  45 us
    pallas_call x1, Pallas kernels, place(): pl.pallas_call(functools.partial(place_kernel, len(held), len(arrays)), o...  4.57 us

profile of v4, /device:TPU:0, one launch (start us, length us, event | category | flops | bytes accessed | tf_op | source)
XLA Modules:
  0.0 51.3 jit_solution(8719858550874025426)
XLA Ops:
  1.3 45.2 %conditional.1 = ((f32[1,2560,128]{2,1,0:T(8,128)S(1)}, f32[1]{0:T(128)}, f32[1,2560,128]{2,1,0:T(8,128)S(1)}, f32[1,2560,128]{2,1,0:T(8,128)}, bf16[1024,128]{1...) conditional(s32[]{:T(128)} %bitcast, (f32[1]{0:T(128)}, bf16[256,2560]{1,0:T(8,128)(2,1)}, ...), branch_computations={%region_0.0_spmd, %region_1.0_spmd, %region_2.0_spmd} | conditional | flops 2013265920 | bytes 12000008 | solution.py:324
  1.3 45.0 %branch_0_fun.1 = (f32[1,2560,128]{2,1,0:T(8,128)S(1)}, f32[1]{0:T(128)}, f32[1,2560,128]{2,1,0:T(8,128)S(1)}, f32[1,2560,128]{2,1,0:T(8,128)}, bf16[1024,128]{1...) custom-call(f32[1]{0:T(128)} %get-tuple-element.36.w_ref, bf16[256,2560]{1,0:T(8,128)(2,1)} %get-tuple-element.37.hid_hbm, ...), custom_call_target="tpu_custom_call" | custom-call | flops 2013265920 | bytes 12000000 | tf_op jit(solution)/shard_map/cond/branch_0_fun/pallas_call | solution.py:267
  46.5 4.6 %shard_map.118 = (f32[1]{0:T(128)}, f32[1,2560,128]{2,1,0:T(8,128)}, f32[1,2560,128]{2,1,0:T(8,128)}, bf16[1024,128]{1,0:T(8,128)(2,1)}, f32[1,2560,128]{2,1,0:T(8,128)}, /*index=5*/bf16[256,2560]{1,0:T(8,128)(2,1)}) custom-call(f32[1]{0:T(128)} %get-tuple-element.72.weight_in, f32[1,2560,128]{2,1,0:T(8,128)S(1)} %get-tuple-element.73.refs_0_, ...), custom_call_target="tpu_custom_call" | custom-call | tf_op jit(solution)/shard_map/pallas_call | solution.py:308

commit v5 on v4

--- a/solution.py
+++ b/solution.py
@@ -40,7 +40,7 @@
         return pl.ds(pl.multiple_of(index * rows, rows), rows)
 
     barrier = pltpu.get_barrier_semaphore()
-    for device in (near_dev, far_dev, to_dev, from_dev):
+    for device in (near_dev, far_dev, from_dev):
         pl.semaphore_signal(barrier, inc=1, device_id=device, device_id_type=MESH)
     loads = [
         pltpu.make_async_copy(num_hbm.at[0], num, load_sem.at[0]),
@@ -55,7 +55,7 @@
     weight = w_ref[0]
     w_send[...] = jnp.full(w_send.shape, weight, F32)
     part = [pl.ds(c * fc, fc) for c in range(chunks)]
-    pl.semaphore_wait(barrier, 4)
+    pl.semaphore_wait(barrier, 3)
 
     def remote(src, dst, send, recv, device):
         return pltpu.make_async_remote_copy(

time: 52 us -> 48.5 us (0.933)
  Pallas kernels: 49.5 us -> 46.5 us
    pallas_call x1, Pallas kernels: 45 us -> 41.9 us  [step_of(): pl.pallas_call(functools.partial(kernel, dist, chunks), out_shape=shapes,...]
where the time goes in v5:
time: 48.5 us; the launch traced here: 48.3 us
  Pallas kernels  46.5 us (96%)
  between operations  1.49 us (3%)
    pallas_call x1, Pallas kernels, step_of(): pl.pallas_call(functools.partial(kernel, dist, chunks), out_shape=shapes,...  41.9 us
    pallas_call x1, Pallas kernels, place(): pl.pallas_call(functools.partial(place_kernel, len(held), len(arrays)), o...  4.57 us

profile of v5, /device:TPU:0, one launch (start us, length us, event | category | flops | bytes accessed | tf_op | source)
XLA Modules:
  0.0 48.3 jit_solution(14799017897130499726)
XLA Ops:
  1.3 42.2 %conditional.1 = ((f32[1,2560,128]{2,1,0:T(8,128)S(1)}, f32[1]{0:T(128)}, f32[1,2560,128]{2,1,0:T(8,128)S(1)}, f32[1,2560,128]{2,1,0:T(8,128)}, bf16[1024,128]{1...) conditional(s32[]{:T(128)} %bitcast, (f32[1]{0:T(128)}, bf16[256,2560]{1,0:T(8,128)(2,1)}, ...), branch_computations={%region_0.0_spmd, %region_1.0_spmd, %region_2.0_spmd} | conditional | flops 2013265920 | bytes 12000008 | solution.py:324
  1.3 41.9 %branch_0_fun.1 = (f32[1,2560,128]{2,1,0:T(8,128)S(1)}, f32[1]{0:T(128)}, f32[1,2560,128]{2,1,0:T(8,128)S(1)}, f32[1,2560,128]{2,1,0:T(8,128)}, bf16[1024,128]{1...) custom-call(f32[1]{0:T(128)} %get-tuple-element.36.w_ref, bf16[256,2560]{1,0:T(8,128)(2,1)} %get-tuple-element.37.hid_hbm, ...), custom_call_target="tpu_custom_call" | custom-call | flops 2013265920 | bytes 12000000 | tf_op jit(solution)/shard_map/cond/branch_0_fun/pallas_call | solution.py:267
  43.5 4.6 %shard_map.118 = (f32[1]{0:T(128)}, f32[1,2560,128]{2,1,0:T(8,128)}, f32[1,2560,128]{2,1,0:T(8,128)}, bf16[1024,128]{1,0:T(8,128)(2,1)}, f32[1,2560,128]{2,1,0:T(8,128)}, /*index=5*/bf16[256,2560]{1,0:T(8,128)(2,1)}) custom-call(f32[1]{0:T(128)} %get-tuple-element.72.weight_in, f32[1,2560,128]{2,1,0:T(8,128)S(1)} %get-tuple-element.73.refs_0_, ...), custom_call_target="tpu_custom_call" | custom-call | tf_op jit(solution)/shard_map/pallas_call | solution.py:308
